TPU v7x, 128 devices: a whole 4x4x4 slice. The times are simulated.
128 devices in a mesh: rng: 8 (over y, x_lo), az: 16 (over x_hi, z, core).
Axes of the slice: x: 4 (x_hi: 2, x_lo: 2; x = x_hi * 2 + x_lo), y: 4, z: 4, core: 2. Of those that a mesh axis runs over, the one named last changes fastest.
Arguments:
- raw_echo: float32 [2, 16384, 4096], P(None, 'az', 'rng'), may hold values from -6 to 6
- chirp_spectrum: float32 [2, 4096], replicated, may hold values from -6 to 6
- azimuth_rate: float32 [4096], P(('rng', 'az')), may hold values from 100 to 400
- shift_table: int32 [16, 4096], P(None, ('rng', 'az')), may hold values from -28 to 29
- filter_index: int32 [16, 4096], P(None, ('rng', 'az')), may hold values from 0 to 15
- tap_table: float32 [16, 8], replicated, may hold values from -3 to 3
Outputs:
- image_out: float32 [2, 4096, 16384], P(None, ('rng', 'az'))
All inputs are finite; a program needn't handle non-finite values.
Results may differ from a plain program's by a relative error of at most 0.0003.
Values sent between devices are 32-bit elements; how exact they have to be, the bound alone decides.
A program may use at most 64 MiB of HBM per device.

v0:
```python
import functools

import jax
import jax.numpy as jnp
import ml_dtypes
import numpy as np
from jax import lax
from jax.experimental import pallas as pl
from jax.experimental.pallas import tpu as pltpu
from jax.sharding import PartitionSpec as P

NRG = 4096
NAZ = 16384
GROUPS = 16
NFILT = 16
TAPS = 8
HALO = 32

NR = 8
NA = 16
NDEV = NR * NA
BINS = NRG // NDEV
LINES = NAZ // NDEV
CHUNKS = 4
CL = LINES // CHUNKS
HALVES = 2
HB = BINS // HALVES
HROWS = NDEV * 2 * HB
BLK = 2 * HB
PAIRS = BINS // 2

F32 = jnp.float32
BF16 = jnp.bfloat16
MESH = pl.DeviceIdType.MESH


def dft_matrix(sign):
    ids = np.arange(128)
    ang = 2.0 * np.pi * (np.outer(ids, ids) % 128) / 128
    c, s = np.cos(ang), sign * np.sin(ang)
    return np.block([[c, -s], [s, c]])


def split_matrix(m):
    hi = m.astype(ml_dtypes.bfloat16)
    lo = (m - hi.astype(np.float64)).astype(ml_dtypes.bfloat16)
    return np.concatenate([hi, hi, lo], axis=1)


def tables():
    wf = split_matrix(dft_matrix(-1.0))
    wi = split_matrix(dft_matrix(1.0))
    wft = np.ascontiguousarray(wf.T)
    k0 = np.arange(32)[:, None]
    b = np.arange(128)[None, :]
    ang = 2.0 * np.pi * (k0 * b % NRG) / NRG
    tw = np.stack([np.cos(ang), -np.sin(ang)])
    tw_in = np.repeat(tw[:, :, None, :], 8, axis=2).astype(np.float32)
    tw_out = np.stack([np.cos(ang), np.sin(ang)])
    tw_out = np.repeat(tw_out.transpose(1, 0, 2)[..., None], 128, axis=3).astype(np.float32)
    ids = np.arange(128)
    ang = 2.0 * np.pi * np.outer(ids, ids) / NAZ
    tw_az = np.stack([np.cos(ang), -np.sin(ang)]).astype(np.float32)
    return wf, wi, wft, tw_in, tw_out, tw_az


def cadd(x, y):
    return (x[0] + y[0], x[1] + y[1])


def csub(x, y):
    return (x[0] - y[0], x[1] - y[1])


def cmul_i(x, sign):
    if sign > 0:
        return (-x[1], x[0])
    return (x[1], -x[0])


def cmul_const(x, num, den, sign):
    num = num % den
    if num == 0:
        return x
    ang = 2.0 * np.pi * num / den
    c, s = float(np.cos(ang)), float(sign * np.sin(ang))
    return (x[0] * c - x[1] * s, x[0] * s + x[1] * c)


def dft4(x, sign):
    a, b = cadd(x[0], x[2]), csub(x[0], x[2])
    c, d = cadd(x[1], x[3]), cmul_i(csub(x[1], x[3]), sign)
    return [cadd(a, c), cadd(b, d), csub(a, c), csub(b, d)]


def dft8(x, sign):
    even = dft4([x[0], x[2], x[4], x[6]], sign)
    odd = dft4([x[1], x[3], x[5], x[7]], sign)
    h = float(np.sqrt(0.5))
    o1 = odd[1]
    o3 = odd[3]
    if sign > 0:
        t1 = ((o1[0] - o1[1]) * h, (o1[0] + o1[1]) * h)
        t3 = ((-o3[0] - o3[1]) * h, (o3[0] - o3[1]) * h)
    else:
        t1 = ((o1[0] + o1[1]) * h, (o1[1] - o1[0]) * h)
        t3 = ((o3[1] - o3[0]) * h, (-o3[0] - o3[1]) * h)
    t = [odd[0], t1, cmul_i(odd[2], sign), t3]
    return [cadd(even[k], t[k]) for k in range(4)] + [csub(even[k], t[k]) for k in range(4)]


def dft32(load, sign):
    cols = []
    for a in range(4):
        y = dft8([load(4 * s + a) for s in range(8)], sign)
        cols.append([cmul_const(y[k], a * k, 32, sign) for k in range(8)])
    out = [None] * 32
    for k in range(8):
        z = dft4([cols[a][k] for a in range(4)], sign)
        for m in range(4):
            out[k + 8 * m] = z[m]
    return out


def three(x, axis):
    hi = x.astype(BF16)
    lo = (x - hi.astype(F32)).astype(BF16)
    return jnp.concatenate([hi, lo, hi], axis=axis)


def dot_nn(a, b):
    return lax.dot_general(a, b, (((1,), (0,)), ((), ())), preferred_element_type=F32)


def dot_nt(a, b):
    return lax.dot_general(a, b, (((1,), (1,)), ((), ())), preferred_element_type=F32)


def dft_pair(w_ref, x, tw_ref, conj):
    y = dot_nn(w_ref[...], three(x, 0))
    tr, ti = tw_ref[0], tw_ref[1]
    if conj:
        ti = -ti
    rows = []
    for m in range(2):
        yr = y[:128, 128 * m : 128 * m + 128]
        yi = y[128:, 128 * m : 128 * m + 128]
        rows.append(jnp.concatenate([yr * tr - yi * ti, yr * ti + yi * tr], axis=1))
    return dot_nt(w_ref[...], three(jnp.concatenate(rows, axis=0), 1))


def half_turns(theta):
    m = jnp.floor(theta + 0.5)
    d = theta - m
    half = m * 0.5
    sign = 1.0 - 4.0 * (half - jnp.floor(half))
    x = d * d
    pi = np.pi
    cs = [float((-1) ** n * pi ** (2 * n) / np.prod(np.arange(1.0, 2 * n + 1))) for n in range(7)]
    sn = [
        float((-1) ** n * pi ** (2 * n + 1) / np.prod(np.arange(1.0, 2 * n + 2))) for n in range(6)
    ]
    c = cs[6]
    for n in range(5, -1, -1):
        c = c * x + cs[n]
    s = sn[5]
    for n in range(4, -1, -1):
        s = s * x + sn[n]
    return c * sign, s * d * sign


def kernel(
    raw, chirp, tw_out_hbm, wf, wi, wft, tw_in, tw_az, rate, shift, filt, taps,
    out,
    xb, ub, cb, db, fb, pb, twb, ob, mb, c2b,
    sem_tw, send1, recv1, send2, recv2, sendh, recvh, sem_out,
):
    i = lax.axis_index("rng")
    j = lax.axis_index("az")
    r = i * NA + j
    q = j * NR + i

    def device(block):
        return (lax.div(block, NA), lax.rem(block, NA))

    barrier = pltpu.get_barrier_semaphore()

    def greet(k, _):
        pl.semaphore_signal(
            barrier, inc=1, device_id=device(lax.rem(r + k, NDEV)), device_id_type=MESH
        )
        return 0

    lax.fori_loop(1, NDEV, greet, 0)
    pl.semaphore_wait(barrier, NDEV - 1)

    for ch in range(CHUNKS):

        def lines(block, ch=ch):
            return pl.ds(pl.multiple_of(block * LINES + ch * CL, CL), CL)

        def send_lines(k, _, ch=ch, lines=lines):
            to = lax.rem(i + k, NR)
            pltpu.make_async_remote_copy(
                src_ref=raw.at[:, lines(to), :],
                dst_ref=xb.at[i, :, pl.ds(ch * CL, CL), :],
                send_sem=send1.at[ch],
                recv_sem=recv1.at[ch],
                device_id=(to, j),
                device_id_type=MESH,
            ).start()
            return 0

        lax.fori_loop(1, NR, send_lines, 0)
        pltpu.make_async_copy(
            raw.at[:, lines(i), :], xb.at[i, :, pl.ds(ch * CL, CL), :], recv1.at[ch]
        ).start()

    tw_copy = pltpu.make_async_copy(tw_out_hbm, twb, sem_tw)
    tw_copy.start()

    f1 = lax.broadcasted_iota(jnp.int32, (128, 128), 0)
    f0 = lax.broadcasted_iota(jnp.int32, (128, 128), 1)
    freq = f0 + 128 * f1
    freq = jnp.where(freq >= NAZ // 2, freq - NAZ, freq)
    c = freq.astype(F32) * (1.0 / NAZ)
    c2b[...] = c * c

    def phases(b, _):
        cosine, sine = half_turns(rate[b] * c2b[...])
        pb[b, 0] = cosine * (1.0 / NAZ)
        pb[b, 1] = sine * (1.0 / NAZ)
        return 0

    lax.fori_loop(0, BINS, phases, 0)

    for ch in range(CHUNKS):
        chunk = xb.at[:, :, pl.ds(ch * CL, CL), :]
        pltpu.make_async_copy(chunk, chunk, recv1.at[ch]).wait()

        def first(t, _, ch=ch):
            rows = pl.ds(pl.multiple_of(ch * CL + t * 8, 8), 8)

            def load(n):
                lanes = pl.ds(128 * (n % 4), 128)
                return (xb[n // 4, 0, rows, lanes], xb[n // 4, 1, rows, lanes])

            res = dft32(load, -1.0)
            for k in range(32):
                lanes = pl.ds(128 * (k % 4), 128)
                tr, ti = tw_in[0, k], tw_in[1, k]
                xr, xi = res[k]
                xb[k // 4, 0, rows, lanes] = xr * tr - xi * ti
                xb[k // 4, 1, rows, lanes] = xr * ti + xi * tr
            return 0

        lax.fori_loop(0, CL // 8, first, 0)

        def second(blk, _, ch=ch):
            rows = pl.ds(ch * CL, CL)
            parts = []
            for m in range(8):
                s = blk * 2 + m // 4
                lanes = pl.ds(128 * (m % 4), 128)
                parts.append(
                    jnp.concatenate([xb[s, 0, rows, lanes], xb[s, 1, rows, lanes]], axis=1)
                )
            y = dot_nn(three(jnp.concatenate(parts, axis=0), 1), wft[...])
            for m in range(8):
                s = blk * 2 + m // 4
                lanes = pl.ds(128 * (m % 4), 128)
                yr = y[m * CL : m * CL + CL, :128]
                yi = y[m * CL : m * CL + CL, 128:]
                hr = chirp[0, pl.ds(blk * 8 + m, 1), :]
                hi = chirp[1, pl.ds(blk * 8 + m, 1), :]
                xb[s, 0, rows, lanes] = yr * hr - yi * hi
                xb[s, 1, rows, lanes] = yr * hi + yi * hr
            return 0

        lax.fori_loop(0, 4, second, 0)

    tw_copy.wait()

    def third(s, _):
        for h in range(2):
            parts = []
            for m in range(2):
                lanes = pl.ds(128 * (2 * h + m), 128)
                parts.append(jnp.concatenate([xb[s, 0, :, lanes], xb[s, 1, :, lanes]], axis=1))
            y = dot_nt(wi[...], three(jnp.concatenate(parts, axis=0), 1))
            for m in range(2):
                k = s * 4 + 2 * h + m
                yr = y[:128, 128 * m : 128 * m + 128]
                yi = y[128:, 128 * m : 128 * m + 128]
                tr, ti = twb[k, 0], twb[k, 1]
                ub[k, 0] = yr * tr - yi * ti
                ub[k, 1] = yr * ti + yi * tr
        return 0

    lax.fori_loop(0, NR, third, 0)

    def make_block(n, _):
        half = lax.div(n, 4)
        beta = lax.rem(n, 4)

        def fourth(t, _):
            rows = pl.ds(pl.multiple_of(32 * beta + HB * half + 8 * t, 8), 8)

            def load(k):
                return (ub[k, 0, rows, :], ub[k, 1, rows, :])

            res = dft32(load, 1.0)
            for a in range(32):
                base = half * HROWS + (4 * a + beta) * BLK + 8 * t
                cb[pl.ds(pl.multiple_of(base, 8), 8), :] = res[a][0]
                cb[pl.ds(pl.multiple_of(base + HB, 8), 8), :] = res[a][1]
            return 0

        lax.fori_loop(0, HB // 8, fourth, 0)
        mine = pl.ds(pl.multiple_of(half * HROWS + q * BLK, 8), BLK)

        def send_block(k, _):
            to = 4 * lax.rem(lax.div(r, 4) + k, 32) + beta
            theirs = pl.ds(pl.multiple_of(half * HROWS + to * BLK, 8), BLK)

            @pl.when(to != r)
            def _():
                pltpu.make_async_remote_copy(
                    src_ref=cb.at[theirs, :],
                    dst_ref=db.at[mine, :],
                    send_sem=send2.at[half],
                    recv_sem=recv2.at[half],
                    device_id=device(to),
                    device_id_type=MESH,
                ).start()

            @pl.when(to == r)
            def _():
                pltpu.make_async_copy(cb.at[theirs, :], db.at[mine, :], recv2.at[half]).start()

            return 0

        lax.fori_loop(0, 32, send_block, 0)
        return 0

    lax.fori_loop(0, 4 * HALVES, make_block, 0)

    up = device(lax.rem(r + 1, NDEV))
    down = device(lax.rem(r + NDEV - 1, NDEV))
    for half in range(HALVES):
        landed = db.at[pl.ds(half * HROWS, HROWS), :]
        pltpu.make_async_copy(landed, landed, recv2.at[half]).wait()

        def azimuth(n, _, half=half):
            base = half * HROWS + 2 * n
            cols = []
            for m in range(2):
                re = db[pl.ds(base + m, 128, stride=BLK), :]
                im = db[pl.ds(base + m + HB, 128, stride=BLK), :]
                cols.append(jnp.concatenate([re, im], axis=0))
            y = dft_pair(wf, jnp.concatenate(cols, axis=1), tw_az, False)
            row = half * HB + 2 * n
            fb[BINS + row] = y[:, :128]
            fb[BINS + row + 1] = y[:, 128:]
            own = fb.at[pl.ds(BINS + row, 2)]
            for place, to, d in ((0, up, 0), (2 * BINS, down, 1)):
                pltpu.make_async_remote_copy(
                    src_ref=own,
                    dst_ref=fb.at[pl.ds(place + row, 2)],
                    send_sem=sendh.at[d],
                    recv_sem=recvh.at[d],
                    device_id=to,
                    device_id_type=MESH,
                ).start()
            return 0

        lax.fori_loop(0, HB // 2, azimuth, 0)

    for d, place in ((0, 0), (1, 2 * BINS)):
        landed = fb.at[pl.ds(place, BINS)]
        pltpu.make_async_copy(landed, landed, recvh.at[d]).wait()

    @pl.when(r == 0)
    def _():
        def clear(n, _):
            fb[n] = jnp.zeros((256, 128), F32)
            return 0

        lax.fori_loop(0, BINS, clear, 0)

    @pl.when(r == NDEV - 1)
    def _():
        def clear(n, _):
            fb[2 * BINS + n] = jnp.zeros((256, 128), F32)
            return 0

        lax.fori_loop(0, BINS, clear, 0)

    def focus(n, _):
        for m in range(2):
            b = 2 * n + m
            lanes = pl.ds(128 * m, 128)
            for g in range(GROUPS):
                first_row = BINS + b + shift[g, b] - 4
                which = filt[g, b]
                re, im = pl.ds(8 * g, 8), pl.ds(128 + 8 * g, 8)
                sr = si = None
                for t in range(TAPS):
                    w = taps[which, t]
                    vr = fb[first_row + t, re, :] * w
                    vi = fb[first_row + t, im, :] * w
                    sr = vr if sr is None else sr + vr
                    si = vi if si is None else si + vi
                pc, ps = pb[b, 0, re, :], pb[b, 1, re, :]
                mb[re, lanes] = sr * pc + si * ps
                mb[im, lanes] = si * pc - sr * ps
        y = dft_pair(wi, mb[...], tw_az, True)
        for m in range(2):
            b = 2 * n + m
            for c in range(2):
                base = (c * 4 + lax.div(b, 8)) * 1024 + lax.rem(b, 8)
                ob[pl.ds(base, 128, stride=8), :] = y[128 * c : 128 * c + 128, 128 * m : 128 * m + 128]
        return 0

    outs = []
    for t in range(4):
        lax.fori_loop(4 * t, 4 * t + 4, focus, 0)
        for c in range(2):
            rows = pl.ds((c * 4 + t) * 1024, 1024)
            copy = pltpu.make_async_copy(ob.at[rows, :], out.at[rows, :], sem_out.at[2 * t + c])
            copy.start()
            outs.append(copy)

    for ch in range(CHUNKS):
        gone = xb.at[pl.ds(0, NR - 1), :, pl.ds(ch * CL, CL), :]
        pltpu.make_async_copy(gone, gone, send1.at[ch]).wait()
    for half in range(HALVES):
        gone = cb.at[pl.ds(0, (NDEV - 1) * BLK), :]
        pltpu.make_async_copy(gone, gone, send2.at[half]).wait()
    for d in range(2):
        gone = fb.at[pl.ds(0, BINS)]
        pltpu.make_async_copy(gone, gone, sendh.at[d]).wait()
    for copy in outs:
        copy.wait()


def local(raw_echo, chirp_spectrum, azimuth_rate, shift_table, filter_index, tap_table):
    wf, wi, wft, tw_in, tw_out, tw_az = tables()
    chirp = chirp_spectrum.reshape(2, 128, 32).transpose(0, 2, 1) * (1.0 / NRG)
    vmem = pl.BlockSpec(memory_space=pltpu.VMEM)
    smem = pl.BlockSpec(memory_space=pltpu.SMEM)
    hbm = pl.BlockSpec(memory_space=pl.ANY)
    dma = pltpu.SemaphoreType.DMA
    image = pl.pallas_call(
        kernel,
        out_shape=jax.ShapeDtypeStruct((8192, 128), F32),
        in_specs=[hbm, vmem, hbm, vmem, vmem, vmem, vmem, vmem, smem, smem, smem, smem],
        out_specs=hbm,
        scratch_shapes=[
            pltpu.VMEM((NR, 2, LINES, 512), F32),
            pltpu.VMEM((32, 2, 128, 128), F32),
            pltpu.VMEM((HALVES * HROWS, 128), F32),
            pltpu.VMEM((HALVES * HROWS, 128), F32),
            pltpu.VMEM((3 * BINS, 256, 128), F32),
            pltpu.VMEM((BINS, 2, 128, 128), F32),
            pltpu.VMEM((32, 2, 128, 128), F32),
            pltpu.VMEM((8192, 128), F32),
            pltpu.VMEM((256, 256), F32),
            pltpu.VMEM((128, 128), F32),
            dma,
            dma((CHUNKS,)),
            dma((CHUNKS,)),
            dma((HALVES,)),
            dma((HALVES,)),
            dma((2,)),
            dma((2,)),
            dma((8,)),
        ],
        compiler_params=pltpu.CompilerParams(
            collective_id=0, has_side_effects=True, vmem_limit_bytes=60 * 1024 * 1024
        ),
        cost_estimate=pl.CostEstimate(
            flops=10_000_000_000, bytes_accessed=16 * 1024 * 1024, transcendentals=0
        ),
        name="focus_slab",
    )(
        raw_echo, chirp, tw_out, wf, wi, wft, tw_in, tw_az,
        azimuth_rate, shift_table, filter_index, tap_table,
    )
    image = image.reshape(2, 4, 128, 8, 128).transpose(0, 1, 3, 2, 4)
    return image.reshape(2, BINS, NAZ)


def solution(mesh):
    return jax.shard_map(
        local,
        mesh=mesh,
        in_specs=(
            P(None, "az", "rng"),
            P(),
            P(("rng", "az")),
            P(None, ("rng", "az")),
            P(None, ("rng", "az")),
            P(),
        ),
        out_specs=P(None, ("rng", "az"), None),
        check_vma=False,
    )
```

profile of v0, /device:TPU:16, one launch (start us, length us, event | category | flops | bytes accessed | tf_op | source)
XLA Modules:
  0.0 219.2 jit_solution(9571567789478389721)
XLA Ops:
  0.0 1.4 copy.15.taps
  1.4 0.8 broadcast_multiply_fusion
  2.1 0.1 mul.12
  2.3 0.7 copy.14
  2.9 211.8 %focus_slab.1 = f32[8192,128]{1,0:T(8,128)} custom-call(f32[2,1024,512]{2,1,0:T(8,128)} %raw.1, f32[2,32,128]{2,1,0:T(8,128)} %bitcast.7, f32[32,2,128,128]{3,2,1,0:T(8,128)} %constant.14.clone.tw_out_hbm, bf16[256,768]{1,0:T(8,128)(2,1)} %constant.15.clone.wf, bf16[256,768]{1,0:T(8,128)(2,1)} %constant.16.clone.wi, bf16[768,256]{1,0:T(8,128)(2,1)} %constant.17.clone.wft, ...), custom_call_target="tpu_custom_call" | custom-call | flops 10000000000 | bytes 16777216 | tf_op jit(solution)/shard_map/focus_slab/pallas_call | solution.py:454
  214.7 4.5 %copy.17 = f32[2,32,16384]{2,1,0:T(8,128)} copy(f32[2,32,16384]{2,1,0:T(8,128)} %bitcast.6) | data formatting | bytes 8388608
where the time goes:
time: 220 us; the launch traced here: 219 us
  Pallas kernels  212 us (96%)
  local copies, waits for them, and re-layouts  6.66 us (3%)
    pallas_call x1, Pallas kernels, local(): pl.pallas_call(kernel, out_shape=jax.ShapeDtypeStruct((8192, 128), F32),...  212 us
    unnamed x2, local copies, waits for them, and re-layouts  5.86 us

commit v1 on v0

--- a/solution.py
+++ b/solution.py
@@ -172,7 +172,7 @@
 def kernel(
     raw, chirp, tw_out_hbm, wf, wi, wft, tw_in, tw_az, rate, shift, filt, taps,
     out,
-    xb, ub, cb, db, fb, pb, twb, ob, mb, c2b,
+    xb, ub, cb, db, fb, pb, twb, mb, c2b,
     sem_tw, send1, recv1, send2, recv2, sendh, recvh, sem_out,
 ):
     i = lax.axis_index("rng")
@@ -293,21 +293,31 @@
                 yr = y[:128, 128 * m : 128 * m + 128]
                 yi = y[128:, 128 * m : 128 * m + 128]
                 tr, ti = twb[k, 0], twb[k, 1]
-                ub[k, 0] = yr * tr - yi * ti
-                ub[k, 1] = yr * ti + yi * tr
+                row = pl.multiple_of(256 * k, 256)
+                ub[pl.ds(row, 128), :] = yr * tr - yi * ti
+                ub[pl.ds(row + 128, 128), :] = yr * ti + yi * tr
         return 0
 
     lax.fori_loop(0, NR, third, 0)
+
+    def shifted(k):
+        zh = lax.rem(lax.div(r, 4) + k + lax.div(k, 16), 2)
+        x = 2 * lax.rem(lax.div(r, 8), 2) + lax.rem(lax.div(r, 16), 2)
+        x = lax.rem(x + k, 4)
+        y = lax.rem(lax.div(r, 32) + k + lax.div(k, 4), 4)
+        return 8 * y + 4 * lax.rem(x, 2) + 2 * lax.div(x, 2) + zh
 
     def make_block(n, _):
         half = lax.div(n, 4)
-        beta = lax.rem(n, 4)
+        beta = (lax.rem(n, 4) + lax.rem(r, 4)) - 2 * (
+            lax.rem(n, 2) * lax.rem(r, 2) + 2 * lax.rem(lax.div(n, 2), 2) * lax.rem(lax.div(r, 2), 2)
+        )
 
         def fourth(t, _):
-            rows = pl.ds(pl.multiple_of(32 * beta + HB * half + 8 * t, 8), 8)
+            row = pl.multiple_of(32 * beta + HB * half + 8 * t, 8)
 
             def load(k):
-                return (ub[k, 0, rows, :], ub[k, 1, rows, :])
+                return (ub[pl.ds(row + 256 * k, 8), :], ub[pl.ds(row + 256 * k + 128, 8), :])
 
             res = dft32(load, 1.0)
             for a in range(32):
@@ -320,7 +330,7 @@
         mine = pl.ds(pl.multiple_of(half * HROWS + q * BLK, 8), BLK)
 
         def send_block(k, _):
-            to = 4 * lax.rem(lax.div(r, 4) + k, 32) + beta
+            to = 4 * shifted(k) + beta
             theirs = pl.ds(pl.multiple_of(half * HROWS + to * BLK, 8), BLK)
 
             @pl.when(to != r)
@@ -347,11 +357,27 @@
 
     up = device(lax.rem(r + 1, NDEV))
     down = device(lax.rem(r + NDEV - 1, NDEV))
+
+    def send_halo(row):
+        own = fb.at[pl.ds(BINS + row, 4)]
+        for place, to, d in ((0, up, 0), (2 * BINS, down, 1)):
+            pltpu.make_async_remote_copy(
+                src_ref=own,
+                dst_ref=fb.at[pl.ds(place + row, 4)],
+                send_sem=sendh.at[d],
+                recv_sem=recvh.at[d],
+                device_id=to,
+                device_id_type=MESH,
+            ).start()
+
     for half in range(HALVES):
         landed = db.at[pl.ds(half * HROWS, HROWS), :]
         pltpu.make_async_copy(landed, landed, recv2.at[half]).wait()
-
-        def azimuth(n, _, half=half):
+        if half == 1:
+            for z in range(4):
+                send_halo(4 * z)
+
+        def azimuth(n, half=half):
             base = half * HROWS + 2 * n
             cols = []
             for m in range(2):
@@ -362,19 +388,15 @@
             row = half * HB + 2 * n
             fb[BINS + row] = y[:, :128]
             fb[BINS + row + 1] = y[:, 128:]
-            own = fb.at[pl.ds(BINS + row, 2)]
-            for place, to, d in ((0, up, 0), (2 * BINS, down, 1)):
-                pltpu.make_async_remote_copy(
-                    src_ref=own,
-                    dst_ref=fb.at[pl.ds(place + row, 2)],
-                    send_sem=sendh.at[d],
-                    recv_sem=recvh.at[d],
-                    device_id=to,
-                    device_id_type=MESH,
-                ).start()
-            return 0
-
-        lax.fori_loop(0, HB // 2, azimuth, 0)
+
+        def azimuth_two(n, _, half=half, azimuth=azimuth):
+            azimuth(2 * n)
+            azimuth(2 * n + 1)
+            if half == 1:
+                send_halo(half * HB + 4 * n)
+            return 0
+
+        lax.fori_loop(0, HB // 4, azimuth_two, 0)
 
     for d, place in ((0, 0), (1, 2 * BINS)):
         landed = fb.at[pl.ds(place, BINS)]
@@ -396,7 +418,7 @@
 
         lax.fori_loop(0, BINS, clear, 0)
 
-    def focus(n, _):
+    def focus(n, mb):
         for m in range(2):
             b = 2 * n + m
             lanes = pl.ds(128 * m, 128)
@@ -419,15 +441,19 @@
             b = 2 * n + m
             for c in range(2):
                 base = (c * 4 + lax.div(b, 8)) * 1024 + lax.rem(b, 8)
-                ob[pl.ds(base, 128, stride=8), :] = y[128 * c : 128 * c + 128, 128 * m : 128 * m + 128]
+                ub[pl.ds(base, 128, stride=8), :] = y[128 * c : 128 * c + 128, 128 * m : 128 * m + 128]
+
+    def focus_two(n, _):
+        focus(2 * n, mb.at[0])
+        focus(2 * n + 1, mb.at[1])
         return 0
 
     outs = []
     for t in range(4):
-        lax.fori_loop(4 * t, 4 * t + 4, focus, 0)
+        lax.fori_loop(2 * t, 2 * t + 2, focus_two, 0)
         for c in range(2):
             rows = pl.ds((c * 4 + t) * 1024, 1024)
-            copy = pltpu.make_async_copy(ob.at[rows, :], out.at[rows, :], sem_out.at[2 * t + c])
+            copy = pltpu.make_async_copy(ub.at[rows, :], out.at[rows, :], sem_out.at[2 * t + c])
             copy.start()
             outs.append(copy)
 
@@ -458,14 +484,13 @@
         out_specs=hbm,
         scratch_shapes=[
             pltpu.VMEM((NR, 2, LINES, 512), F32),
-            pltpu.VMEM((32, 2, 128, 128), F32),
+            pltpu.VMEM((8192, 128), F32),
             pltpu.VMEM((HALVES * HROWS, 128), F32),
             pltpu.VMEM((HALVES * HROWS, 128), F32),
             pltpu.VMEM((3 * BINS, 256, 128), F32),
             pltpu.VMEM((BINS, 2, 128, 128), F32),
             pltpu.VMEM((32, 2, 128, 128), F32),
-            pltpu.VMEM((8192, 128), F32),
-            pltpu.VMEM((256, 256), F32),
+            pltpu.VMEM((2, 256, 256), F32),
             pltpu.VMEM((128, 128), F32),
             dma,
             dma((CHUNKS,)),

time: 220 us -> 185 us (0.84)
  Pallas kernels: 212 us -> 175 us
    pallas_call x1, Pallas kernels: 212 us -> 175 us  [local(): pl.pallas_call(kernel, out_shape=jax.ShapeDtypeStruct((8192, 128), F32),...]
where the time goes in v1:
time: 185 us; the launch traced here: 183 us
  Pallas kernels  175 us (95%)
  local copies, waits for them, and re-layouts  6.66 us (4%)
    pallas_call x1, Pallas kernels, local(): pl.pallas_call(kernel, out_shape=jax.ShapeDtypeStruct((8192, 128), F32),...  175 us
    unnamed x2, local copies, waits for them, and re-layouts  5.86 us

profile of v1, /device:TPU:16, one launch (start us, length us, event | category | flops | bytes accessed | tf_op | source)
XLA Modules:
  0.0 182.7 jit_solution(554048121454589644)
XLA Ops:
  0.0 1.4 copy.15.taps
  1.4 0.8 broadcast_multiply_fusion
  2.1 0.1 mul.12
  2.3 0.7 copy.14
  2.9 175.2 %focus_slab.1 = f32[8192,128]{1,0:T(8,128)} custom-call(f32[2,1024,512]{2,1,0:T(8,128)} %raw.1, f32[2,32,128]{2,1,0:T(8,128)} %bitcast.7, f32[32,2,128,128]{3,2,1,0:T(8,128)} %constant.14.clone.tw_out_hbm, bf16[256,768]{1,0:T(8,128)(2,1)} %constant.15.clone.wf, bf16[256,768]{1,0:T(8,128)(2,1)} %constant.16.clone.wi, bf16[768,256]{1,0:T(8,128)(2,1)} %constant.17.clone.wft, ...), custom_call_target="tpu_custom_call" | custom-call | flops 10000000000 | bytes 16777216 | tf_op jit(solution)/shard_map/focus_slab/pallas_call | solution.py:480
  178.2 4.5 %copy.17 = f32[2,32,16384]{2,1,0:T(8,128)} copy(f32[2,32,16384]{2,1,0:T(8,128)} %bitcast.6) | data formatting | bytes 8388608

commit v2 on v0

--- a/solution.py
+++ b/solution.py
@@ -24,10 +24,11 @@
 CHUNKS = 4
 CL = LINES // CHUNKS
 HALVES = 2
+HL = LINES // HALVES
 HB = BINS // HALVES
-HROWS = NDEV * 2 * HB
-BLK = 2 * HB
-PAIRS = BINS // 2
+COL = 8
+PLANE = 16
+QROWS = 2048
 
 F32 = jnp.float32
 BF16 = jnp.bfloat16
@@ -51,17 +52,21 @@
     wf = split_matrix(dft_matrix(-1.0))
     wi = split_matrix(dft_matrix(1.0))
     wft = np.ascontiguousarray(wf.T)
+    y, xl, xh, zc = np.meshgrid(np.arange(4), np.arange(2), np.arange(2), np.arange(8), indexing="ij")
+    order = (64 * xh + 8 * zc + 2 * y + xl).reshape(-1)
+    wq = split_matrix(dft_matrix(-1.0)[:, np.concatenate([order, order + 128])])
     k0 = np.arange(32)[:, None]
     b = np.arange(128)[None, :]
     ang = 2.0 * np.pi * (k0 * b % NRG) / NRG
     tw = np.stack([np.cos(ang), -np.sin(ang)])
     tw_in = np.repeat(tw[:, :, None, :], 8, axis=2).astype(np.float32)
-    tw_out = np.stack([np.cos(ang), np.sin(ang)])
-    tw_out = np.repeat(tw_out.transpose(1, 0, 2)[..., None], 128, axis=3).astype(np.float32)
+    tw_out = np.stack([np.cos(ang), np.sin(ang)], axis=1)
+    tw_out = tw_out.reshape(32, 2, 8, 2, 8).transpose(0, 1, 2, 4, 3).reshape(32, 2, 64, 2)
+    tw_out = np.repeat(tw_out, HL, axis=3).astype(np.float32)
     ids = np.arange(128)
     ang = 2.0 * np.pi * np.outer(ids, ids) / NAZ
     tw_az = np.stack([np.cos(ang), -np.sin(ang)]).astype(np.float32)
-    return wf, wi, wft, tw_in, tw_out, tw_az
+    return wf, wi, wft, wq, tw_in, tw_out, tw_az
 
 
 def cadd(x, y):
@@ -136,8 +141,15 @@
     return lax.dot_general(a, b, (((1,), (1,)), ((), ())), preferred_element_type=F32)
 
 
-def dft_pair(w_ref, x, tw_ref, conj):
-    y = dot_nn(w_ref[...], three(x, 0))
+def swap_halves(x, y):
+    low = lax.broadcasted_iota(jnp.int32, x.shape, 1) < 64
+    return jnp.where(low, x, pltpu.roll(y, 64, 1)), jnp.where(low, pltpu.roll(x, 64, 1), y)
+
+
+def dft_pair(w_first, w_ref, x, tw_ref, conj, mixed=False):
+    y = dot_nn(w_first[...], three(x, 0))
+    if mixed:
+        y = jnp.concatenate(swap_halves(y[:, :128], y[:, 128:]), axis=1)
     tr, ti = tw_ref[0], tw_ref[1]
     if conj:
         ti = -ti
@@ -170,29 +182,56 @@
 
 
 def kernel(
-    raw, chirp, tw_out_hbm, wf, wi, wft, tw_in, tw_az, rate, shift, filt, taps,
+    raw, chirp, tw_out_hbm, wf, wi, wft, wq, tw_in, tw_az, rate, shift, filt, taps,
     out,
-    xb, ub, cb, db, fb, pb, twb, ob, mb, c2b,
-    sem_tw, send1, recv1, send2, recv2, sendh, recvh, sem_out,
+    xb, ub, cb, eb, db, fb, pb, twb, mb, c2b,
+    sem_tw, send1, recv1, sendz, recvz, sendy, recvy, sendh, recvh, sem_out,
 ):
     i = lax.axis_index("rng")
     j = lax.axis_index("az")
     r = i * NA + j
     q = j * NR + i
 
+    zc = lax.rem(j, COL)
+    xh = lax.div(j, COL)
+    xl = lax.rem(i, 2)
+    y = lax.div(i, 2)
+    x = 2 * xh + xl
+    yx = 4 * y + 2 * xl + xh
+
     def device(block):
         return (lax.div(block, NA), lax.rem(block, NA))
 
+    def in_column(k):
+        return lax.rem(zc + k, COL)
+
+    def in_plane(k):
+        to_x = lax.rem(x + k, 4)
+        to_y = lax.rem(y + k + lax.div(k, 4), 4)
+        to_xl, to_xh = lax.rem(to_x, 2), lax.div(to_x, 2)
+        return 4 * to_y + 2 * to_xl + to_xh, (2 * to_y + to_xl, COL * to_xh + zc)
+
+    up = device(lax.rem(r + 1, NDEV))
+    down = device(lax.rem(r + NDEV - 1, NDEV))
+
     barrier = pltpu.get_barrier_semaphore()
 
-    def greet(k, _):
-        pl.semaphore_signal(
-            barrier, inc=1, device_id=device(lax.rem(r + k, NDEV)), device_id_type=MESH
-        )
+    def greet(to):
+        pl.semaphore_signal(barrier, inc=1, device_id=to, device_id_type=MESH)
+
+    def greet_column(k, _):
+        greet((i, COL * xh + in_column(k)))
         return 0
 
-    lax.fori_loop(1, NDEV, greet, 0)
-    pl.semaphore_wait(barrier, NDEV - 1)
+    def greet_plane(k, _):
+        greet(in_plane(k)[1])
+        return 0
+
+    lax.fori_loop(1, PLANE, greet_plane, 0)
+    lax.fori_loop(1, COL, greet_column, 0)
+    greet(up)
+    greet(down)
+    pl.semaphore_wait(barrier, PLANE - 1 + COL - 1 + 2)
 
     for ch in range(CHUNKS):
 
@@ -234,7 +273,7 @@
 
     lax.fori_loop(0, BINS, phases, 0)
 
-    for ch in range(CHUNKS):
+    def first_two(ch):
         chunk = xb.at[:, :, pl.ds(ch * CL, CL), :]
         pltpu.make_async_copy(chunk, chunk, recv1.at[ch]).wait()
 
@@ -279,91 +318,117 @@
 
         lax.fori_loop(0, 4, second, 0)
 
-    tw_copy.wait()
-
-    def third(s, _):
-        for h in range(2):
+    def third(half):
+        lines = pl.ds(half * HL, HL)
+
+        def step(n, _):
             parts = []
-            for m in range(2):
-                lanes = pl.ds(128 * (2 * h + m), 128)
-                parts.append(jnp.concatenate([xb[s, 0, :, lanes], xb[s, 1, :, lanes]], axis=1))
+            for m in range(4):
+                lanes = pl.ds(128 * m, 128)
+                parts.append(
+                    jnp.concatenate([xb[n, 0, lines, lanes], xb[n, 1, lines, lanes]], axis=1)
+                )
             y = dot_nt(wi[...], three(jnp.concatenate(parts, axis=0), 1))
-            for m in range(2):
-                k = s * 4 + 2 * h + m
-                yr = y[:128, 128 * m : 128 * m + 128]
-                yi = y[128:, 128 * m : 128 * m + 128]
-                tr, ti = twb[k, 0], twb[k, 1]
-                ub[k, 0] = yr * tr - yi * ti
-                ub[k, 1] = yr * ti + yi * tr
-        return 0
-
-    lax.fori_loop(0, NR, third, 0)
-
-    def make_block(n, _):
-        half = lax.div(n, 4)
-        beta = lax.rem(n, 4)
-
-        def fourth(t, _):
-            rows = pl.ds(pl.multiple_of(32 * beta + HB * half + 8 * t, 8), 8)
+            for h in range(2):
+                z = y[:, 128 * h : 128 * h + 128].reshape(16, 2, 8, 128)
+                pair = swap_halves(z[:, 0].reshape(128, 128), z[:, 1].reshape(128, 128))
+                for m in range(2):
+                    k = n * 4 + 2 * h + m
+                    zr, zi = pair[m][:64], pair[m][64:]
+                    tr, ti = twb[k, 0], twb[k, 1]
+                    row = pl.multiple_of(128 * k, 128)
+                    ub[pl.ds(row, 64), :] = zr * tr - zi * ti
+                    ub[pl.ds(row + 64, 64), :] = zr * ti + zi * tr
+            return 0
+
+        lax.fori_loop(0, NR, step, 0)
+
+    def fourth(half, part):
+        quarter = 2 * half + part
+
+        def step(n, _):
+            own = lax.rem(r, 4)
+            beta = (n + own) - 2 * (
+                lax.rem(n, 2) * lax.rem(own, 2) + 2 * lax.div(n, 2) * lax.div(own, 2)
+            )
+            row = pl.multiple_of(8 * (2 * beta + part), 8)
 
             def load(k):
-                return (ub[k, 0, rows, :], ub[k, 1, rows, :])
+                return (ub[pl.ds(row + 128 * k, 8), :], ub[pl.ds(row + 128 * k + 64, 8), :])
 
             res = dft32(load, 1.0)
             for a in range(32):
-                base = half * HROWS + (4 * a + beta) * BLK + 8 * t
+                base = quarter * QROWS + (4 * (a % 2) + beta) * 256 + (a // 2) * 16
                 cb[pl.ds(pl.multiple_of(base, 8), 8), :] = res[a][0]
-                cb[pl.ds(pl.multiple_of(base + HB, 8), 8), :] = res[a][1]
-            return 0
-
-        lax.fori_loop(0, HB // 8, fourth, 0)
-        mine = pl.ds(pl.multiple_of(half * HROWS + q * BLK, 8), BLK)
-
-        def send_block(k, _):
-            to = 4 * lax.rem(lax.div(r, 4) + k, 32) + beta
-            theirs = pl.ds(pl.multiple_of(half * HROWS + to * BLK, 8), BLK)
-
-            @pl.when(to != r)
-            def _():
-                pltpu.make_async_remote_copy(
-                    src_ref=cb.at[theirs, :],
-                    dst_ref=db.at[mine, :],
-                    send_sem=send2.at[half],
-                    recv_sem=recv2.at[half],
-                    device_id=device(to),
-                    device_id_type=MESH,
-                ).start()
-
-            @pl.when(to == r)
-            def _():
-                pltpu.make_async_copy(cb.at[theirs, :], db.at[mine, :], recv2.at[half]).start()
-
-            return 0
-
-        lax.fori_loop(0, 32, send_block, 0)
-        return 0
-
-    lax.fori_loop(0, 4 * HALVES, make_block, 0)
-
-    up = device(lax.rem(r + 1, NDEV))
-    down = device(lax.rem(r + NDEV - 1, NDEV))
-    for half in range(HALVES):
-        landed = db.at[pl.ds(half * HROWS, HROWS), :]
-        pltpu.make_async_copy(landed, landed, recv2.at[half]).wait()
-
-        def azimuth(n, _, half=half):
-            base = half * HROWS + 2 * n
-            cols = []
-            for m in range(2):
-                re = db[pl.ds(base + m, 128, stride=BLK), :]
-                im = db[pl.ds(base + m + HB, 128, stride=BLK), :]
-                cols.append(jnp.concatenate([re, im], axis=0))
-            y = dft_pair(wf, jnp.concatenate(cols, axis=1), tw_az, False)
-            row = half * HB + 2 * n
-            fb[BINS + row] = y[:, :128]
-            fb[BINS + row + 1] = y[:, 128:]
-            own = fb.at[pl.ds(BINS + row, 2)]
-            for place, to, d in ((0, up, 0), (2 * BINS, down, 1)):
+                cb[pl.ds(pl.multiple_of(base + 8, 8), 8), :] = res[a][1]
+            for zh in range(2):
+                to = 4 * zh + beta
+                rows = pl.ds(pl.multiple_of(quarter * QROWS + to * 256, 256), 256)
+                place = eb.at[quarter * COL + zc]
+
+                @pl.when(to != zc)
+                def _(rows=rows, to=to, place=place):
+                    pltpu.make_async_remote_copy(
+                        src_ref=cb.at[rows, :],
+                        dst_ref=place,
+                        send_sem=sendz.at[quarter],
+                        recv_sem=recvz.at[quarter],
+                        device_id=(i, COL * xh + to),
+                        device_id_type=MESH,
+                    ).start()
+
+                @pl.when(to == zc)
+                def _(rows=rows, place=place):
+                    pltpu.make_async_copy(cb.at[rows, :], place, recvz.at[quarter]).start()
+
+            return 0
+
+        lax.fori_loop(0, 4, step, 0)
+
+    def forward(half, part):
+        quarter = 2 * half + part
+        landed = eb.at[pl.ds(quarter * COL, COL)]
+        pltpu.make_async_copy(landed, landed, recvz.at[quarter]).wait()
+        place = db.at[pl.ds(quarter * 128 + yx * COL, COL)]
+
+        def send(k, _):
+            to, to_device = in_plane(k)
+            pltpu.make_async_remote_copy(
+                src_ref=landed.at[:, pl.ds(pl.multiple_of(to * 16, 16), 16), :],
+                dst_ref=place,
+                send_sem=sendy.at[quarter],
+                recv_sem=recvy.at[quarter],
+                device_id=to_device,
+                device_id_type=MESH,
+            ).start()
+            return 0
+
+        lax.fori_loop(1, PLANE, send, 0)
+        pltpu.make_async_copy(
+            landed.at[:, pl.ds(pl.multiple_of(yx * 16, 16), 16), :], place, recvy.at[quarter]
+        ).start()
+
+    first_two(0)
+    first_two(1)
+    tw_copy.wait()
+    third(0)
+    fourth(0, 0)
+    fourth(0, 1)
+    first_two(2)
+    forward(0, 0)
+    first_two(3)
+    forward(0, 1)
+    third(1)
+    fourth(1, 0)
+    fourth(1, 1)
+    forward(1, 0)
+    forward(1, 1)
+
+    def send_halo(row, inner, cross):
+        own = fb.at[pl.ds(BINS + row, 2)]
+        for place, to, d, edge in ((0, up, 0, COL - 1), (2 * BINS, down, 1, 0)):
+
+            def go(place=place, to=to, d=d):
                 pltpu.make_async_remote_copy(
                     src_ref=own,
                     dst_ref=fb.at[pl.ds(place + row, 2)],
@@ -372,9 +437,43 @@
                     device_id=to,
                     device_id_type=MESH,
                 ).start()
-            return 0
-
-        lax.fori_loop(0, HB // 2, azimuth, 0)
+
+            if inner and cross:
+                go()
+            elif inner:
+                pl.when(zc != edge)(go)
+            else:
+                pl.when(zc == edge)(go)
+
+    flat = db.reshape(HALVES * HALVES * QROWS, 128)
+    for part in range(HALVES):
+        for half in range(HALVES):
+            landed = db.at[pl.ds((2 * half + part) * 128, 128)]
+            pltpu.make_async_copy(landed, landed, recvy.at[2 * half + part]).wait()
+        if part == 1:
+            for z in range(8):
+                send_halo(2 * z, False, True)
+
+        def azimuth(n, part=part):
+            cols = []
+            for half in range(HALVES):
+                base = (2 * half + part) * QROWS + n
+                re = flat[pl.ds(base, 128, stride=16), :]
+                im = flat[pl.ds(base + 8, 128, stride=16), :]
+                cols.append(jnp.concatenate([re, im], axis=0))
+            out_pair = dft_pair(wq, wf, jnp.concatenate(cols, axis=1), tw_az, False, mixed=True)
+            row = BINS + part * HB + n
+            fb[row] = out_pair[:, :128]
+            fb[row + 8] = out_pair[:, 128:]
+
+        def azimuth_two(n, _, part=part, azimuth=azimuth):
+            azimuth(2 * n)
+            azimuth(2 * n + 1)
+            send_halo(part * HB + 2 * n, True, part == 1)
+            send_halo(part * HB + 2 * n + 8, True, part == 1)
+            return 0
+
+        lax.fori_loop(0, HB // 4, azimuth_two, 0)
 
     for d, place in ((0, 0), (1, 2 * BINS)):
         landed = fb.at[pl.ds(place, BINS)]
@@ -396,7 +495,7 @@
 
         lax.fori_loop(0, BINS, clear, 0)
 
-    def focus(n, _):
+    def focus(n, mb):
         for m in range(2):
             b = 2 * n + m
             lanes = pl.ds(128 * m, 128)
@@ -406,7 +505,7 @@
                 re, im = pl.ds(8 * g, 8), pl.ds(128 + 8 * g, 8)
                 sr = si = None
                 for t in range(TAPS):
-                    w = taps[which, t]
+                    w = taps[t, which]
                     vr = fb[first_row + t, re, :] * w
                     vi = fb[first_row + t, im, :] * w
                     sr = vr if sr is None else sr + vr
@@ -414,29 +513,35 @@
                 pc, ps = pb[b, 0, re, :], pb[b, 1, re, :]
                 mb[re, lanes] = sr * pc + si * ps
                 mb[im, lanes] = si * pc - sr * ps
-        y = dft_pair(wi, mb[...], tw_az, True)
+        y = dft_pair(wi, wi, mb[...], tw_az, True)
         for m in range(2):
             b = 2 * n + m
             for c in range(2):
                 base = (c * 4 + lax.div(b, 8)) * 1024 + lax.rem(b, 8)
-                ob[pl.ds(base, 128, stride=8), :] = y[128 * c : 128 * c + 128, 128 * m : 128 * m + 128]
+                ub[pl.ds(base, 128, stride=8), :] = y[128 * c : 128 * c + 128, 128 * m : 128 * m + 128]
+
+    def focus_two(n, _):
+        focus(2 * n, mb.at[0])
+        focus(2 * n + 1, mb.at[1])
         return 0
 
     outs = []
     for t in range(4):
-        lax.fori_loop(4 * t, 4 * t + 4, focus, 0)
+        lax.fori_loop(2 * t, 2 * t + 2, focus_two, 0)
         for c in range(2):
             rows = pl.ds((c * 4 + t) * 1024, 1024)
-            copy = pltpu.make_async_copy(ob.at[rows, :], out.at[rows, :], sem_out.at[2 * t + c])
+            copy = pltpu.make_async_copy(ub.at[rows, :], out.at[rows, :], sem_out.at[2 * t + c])
             copy.start()
             outs.append(copy)
 
     for ch in range(CHUNKS):
         gone = xb.at[pl.ds(0, NR - 1), :, pl.ds(ch * CL, CL), :]
         pltpu.make_async_copy(gone, gone, send1.at[ch]).wait()
-    for half in range(HALVES):
-        gone = cb.at[pl.ds(0, (NDEV - 1) * BLK), :]
-        pltpu.make_async_copy(gone, gone, send2.at[half]).wait()
+    for quarter in range(4):
+        gone = cb.at[pl.ds(0, (COL - 1) * 256), :]
+        pltpu.make_async_copy(gone, gone, sendz.at[quarter]).wait()
+        gone = eb.at[pl.ds(0, COL), pl.ds(0, (PLANE - 1) * 16), :]
+        pltpu.make_async_copy(gone, gone, sendy.at[quarter]).wait()
     for d in range(2):
         gone = fb.at[pl.ds(0, BINS)]
         pltpu.make_async_copy(gone, gone, sendh.at[d]).wait()
@@ -445,7 +550,7 @@
 
 
 def local(raw_echo, chirp_spectrum, azimuth_rate, shift_table, filter_index, tap_table):
-    wf, wi, wft, tw_in, tw_out, tw_az = tables()
+    wf, wi, wft, wq, tw_in, tw_out, tw_az = tables()
     chirp = chirp_spectrum.reshape(2, 128, 32).transpose(0, 2, 1) * (1.0 / NRG)
     vmem = pl.BlockSpec(memory_space=pltpu.VMEM)
     smem = pl.BlockSpec(memory_space=pltpu.SMEM)
@@ -454,24 +559,26 @@
     image = pl.pallas_call(
         kernel,
         out_shape=jax.ShapeDtypeStruct((8192, 128), F32),
-        in_specs=[hbm, vmem, hbm, vmem, vmem, vmem, vmem, vmem, smem, smem, smem, smem],
+        in_specs=[hbm, vmem, hbm, vmem, vmem, vmem, vmem, vmem, vmem, smem, smem, smem, smem],
         out_specs=hbm,
         scratch_shapes=[
             pltpu.VMEM((NR, 2, LINES, 512), F32),
-            pltpu.VMEM((32, 2, 128, 128), F32),
-            pltpu.VMEM((HALVES * HROWS, 128), F32),
-            pltpu.VMEM((HALVES * HROWS, 128), F32),
+            pltpu.VMEM((8192, 128), F32),
+            pltpu.VMEM((4 * QROWS, 128), F32),
+            pltpu.VMEM((4 * COL, 256, 128), F32),
+            pltpu.VMEM((512, 16, 128), F32),
             pltpu.VMEM((3 * BINS, 256, 128), F32),
             pltpu.VMEM((BINS, 2, 128, 128), F32),
-            pltpu.VMEM((32, 2, 128, 128), F32),
-            pltpu.VMEM((8192, 128), F32),
-            pltpu.VMEM((256, 256), F32),
+            pltpu.VMEM((32, 2, 64, 128), F32),
+            pltpu.VMEM((2, 256, 256), F32),
             pltpu.VMEM((128, 128), F32),
             dma,
             dma((CHUNKS,)),
             dma((CHUNKS,)),
-            dma((HALVES,)),
-            dma((HALVES,)),
+            dma((4,)),
+            dma((4,)),
+            dma((4,)),
+            dma((4,)),
             dma((2,)),
             dma((2,)),
             dma((8,)),
@@ -484,8 +591,8 @@
         ),
         name="focus_slab",
     )(
-        raw_echo, chirp, tw_out, wf, wi, wft, tw_in, tw_az,
-        azimuth_rate, shift_table, filter_index, tap_table,
+        raw_echo, chirp, tw_out, wf, wi, wft, wq, tw_in, tw_az,
+        azimuth_rate, shift_table, filter_index, tap_table.T,
     )
     image = image.reshape(2, 4, 128, 8, 128).transpose(0, 1, 3, 2, 4)
     return image.reshape(2, BINS, NAZ)

time: 220 us -> 176 us (0.80)
  Pallas kernels: 212 us -> 169 us
    pallas_call x1, Pallas kernels: 212 us -> 169 us  [local(): pl.pallas_call(kernel, out_shape=jax.ShapeDtypeStruct((8192, 128), F32),...]
    unnamed x2 -> x1, local copies, waits for them, and re-layouts: 5.86 us -> 4.5 us
where the time goes in v2:
time: 176 us; the launch traced here: 175 us
  Pallas kernels  169 us (96%)
  local copies, waits for them, and re-layouts  5.31 us (3%)
    pallas_call x1, Pallas kernels, local(): pl.pallas_call(kernel, out_shape=jax.ShapeDtypeStruct((8192, 128), F32),...  169 us
    unnamed x1, local copies, waits for them, and re-layouts  4.5 us

profile of v2, /device:TPU:16, one launch (start us, length us, event | category | flops | bytes accessed | tf_op | source)
XLA Modules:
  0.0 174.9 jit_solution(5110728460682843987)
XLA Ops:
  0.0 0.8 broadcast_multiply_fusion
  0.8 0.1 mul.12
  0.9 0.7 copy.14
  1.6 168.8 %focus_slab.1 = f32[8192,128]{1,0:T(8,128)} custom-call(f32[2,1024,512]{2,1,0:T(8,128)} %raw.1, f32[2,32,128]{2,1,0:T(8,128)} %bitcast.8, f32[32,2,64,128]{3,2,1,0:T(8,128)} %constant.16.clone.tw_out_hbm, bf16[256,768]{1,0:T(8,128)(2,1)} %constant.17.clone.wf, bf16[256,768]{1,0:T(8,128)(2,1)} %constant.18.clone.wi, bf16[768,256]{1,0:T(8,128)(2,1)} %constant.19.clone.wft, ...), custom_call_target="tpu_custom_call" | custom-call | flops 10000000000 | bytes 16777216 | tf_op jit(solution)/shard_map/focus_slab/pallas_call | solution.py:559
  170.4 4.5 %copy.16 = f32[2,32,16384]{2,1,0:T(8,128)} copy(f32[2,32,16384]{2,1,0:T(8,128)} %bitcast.7) | data formatting | bytes 8388608

commit v3 on v2

--- a/solution.py
+++ b/solution.py
@@ -51,7 +51,12 @@
 def tables():
     wf = split_matrix(dft_matrix(-1.0))
     wi = split_matrix(dft_matrix(1.0))
-    wft = np.ascontiguousarray(wf.T)
+    lane = np.arange(128)
+    k1 = 4 * (lane % 32) + lane // 32
+    k1 = np.concatenate([k1, k1 + 128])
+    wft = np.ascontiguousarray(split_matrix(dft_matrix(-1.0)[k1]).T)
+    b = np.arange(128).reshape(8, 8, 2).transpose(0, 2, 1).reshape(-1)
+    wr = split_matrix(dft_matrix(1.0)[np.concatenate([b, b + 128])][:, k1])
     y, xl, xh, zc = np.meshgrid(np.arange(4), np.arange(2), np.arange(2), np.arange(8), indexing="ij")
     order = (64 * xh + 8 * zc + 2 * y + xl).reshape(-1)
     wq = split_matrix(dft_matrix(-1.0)[:, np.concatenate([order, order + 128])])
@@ -61,12 +66,12 @@
     tw = np.stack([np.cos(ang), -np.sin(ang)])
     tw_in = np.repeat(tw[:, :, None, :], 8, axis=2).astype(np.float32)
     tw_out = np.stack([np.cos(ang), np.sin(ang)], axis=1)
-    tw_out = tw_out.reshape(32, 2, 8, 2, 8).transpose(0, 1, 2, 4, 3).reshape(32, 2, 64, 2)
+    tw_out = tw_out.reshape(32, 2, 64, 2)
     tw_out = np.repeat(tw_out, HL, axis=3).astype(np.float32)
     ids = np.arange(128)
     ang = 2.0 * np.pi * np.outer(ids, ids) / NAZ
     tw_az = np.stack([np.cos(ang), -np.sin(ang)]).astype(np.float32)
-    return wf, wi, wft, wq, tw_in, tw_out, tw_az
+    return wf, wi, wft, wr, wq, tw_in, tw_out, tw_az
 
 
 def cadd(x, y):
@@ -182,10 +187,10 @@
 
 
 def kernel(
-    raw, chirp, tw_out_hbm, wf, wi, wft, wq, tw_in, tw_az, rate, shift, filt, taps,
+    raw, spectrum, tw_out_hbm, wf, wi, wft, wr, wq, tw_in, tw_az, rate, shift, filt, taps,
     out,
-    xb, ub, cb, eb, db, fb, pb, twb, mb, c2b,
-    sem_tw, send1, recv1, sendz, recvz, sendy, recvy, sendh, recvh, sem_out,
+    xb, ub, cb, eb, db, fb, lb, pb, twb, mb, c2b, chirp,
+    sem_tw, send1, recv1, sendz, recvz, sendy, recvy, sendn, recvn, sendf, recvf, sem_out,
 ):
     i = lax.axis_index("rng")
     j = lax.axis_index("az")
@@ -197,6 +202,7 @@
     xl = lax.rem(i, 2)
     y = lax.div(i, 2)
     x = 2 * xh + xl
+    core = lax.rem(j, 2)
     yx = 4 * y + 2 * xl + xh
 
     def device(block):
@@ -211,8 +217,12 @@
         to_xl, to_xh = lax.rem(to_x, 2), lax.div(to_x, 2)
         return 4 * to_y + 2 * to_xl + to_xh, (2 * to_y + to_xl, COL * to_xh + zc)
 
-    up = device(lax.rem(r + 1, NDEV))
-    down = device(lax.rem(r + NDEV - 1, NDEV))
+    near = (i, j + 1 - 2 * core)
+    far = device(lax.rem(r + NDEV + 2 * core - 1, NDEV))
+    leaves = jnp.logical_or(zc == 0, zc == COL - 1)
+
+    def turned(n, last, flip):
+        return n + flip * (last - 2 * n)
 
     barrier = pltpu.get_barrier_semaphore()
 
@@ -229,9 +239,8 @@
 
     lax.fori_loop(1, PLANE, greet_plane, 0)
     lax.fori_loop(1, COL, greet_column, 0)
-    greet(up)
-    greet(down)
-    pl.semaphore_wait(barrier, PLANE - 1 + COL - 1 + 2)
+    greet(far)
+    pl.semaphore_wait(barrier, PLANE - 1 + COL - 1 + 1)
 
     for ch in range(CHUNKS):
 
@@ -257,6 +266,14 @@
 
     tw_copy = pltpu.make_async_copy(tw_out_hbm, twb, sem_tw)
     tw_copy.start()
+
+    for part in range(2):
+        rows = [spectrum[part : part + 1, 128 * n : 128 * n + 128] for n in range(32)]
+        tall = jnp.concatenate(rows + [jnp.zeros((96, 128), F32)], axis=0).T
+        spread = tall[:32]
+        for n in range(1, 4):
+            spread = spread + pltpu.roll(tall[32 * n : 32 * n + 32], 32 * n, 1)
+        chirp[part] = spread * (1.0 / NRG)
 
     f1 = lax.broadcasted_iota(jnp.int32, (128, 128), 0)
     f0 = lax.broadcasted_iota(jnp.int32, (128, 128), 1)
@@ -328,7 +345,7 @@
                 parts.append(
                     jnp.concatenate([xb[n, 0, lines, lanes], xb[n, 1, lines, lanes]], axis=1)
                 )
-            y = dot_nt(wi[...], three(jnp.concatenate(parts, axis=0), 1))
+            y = dot_nt(wr[...], three(jnp.concatenate(parts, axis=0), 1))
             for h in range(2):
                 z = y[:, 128 * h : 128 * h + 128].reshape(16, 2, 8, 128)
                 pair = swap_halves(z[:, 0].reshape(128, 128), z[:, 1].reshape(128, 128))
@@ -351,7 +368,8 @@
             beta = (n + own) - 2 * (
                 lax.rem(n, 2) * lax.rem(own, 2) + 2 * lax.div(n, 2) * lax.div(own, 2)
             )
-            row = pl.multiple_of(8 * (2 * beta + part), 8)
+            to_core = lax.rem(beta, 2)
+            row = pl.multiple_of(8 * (2 * beta + part + to_core - 2 * part * to_core), 8)
 
             def load(k):
                 return (ub[pl.ds(row + 128 * k, 8), :], ub[pl.ds(row + 128 * k + 64, 8), :])
@@ -424,76 +442,73 @@
     forward(1, 0)
     forward(1, 1)
 
-    def send_halo(row, inner, cross):
-        own = fb.at[pl.ds(BINS + row, 2)]
-        for place, to, d, edge in ((0, up, 0, COL - 1), (2 * BINS, down, 1, 0)):
-
-            def go(place=place, to=to, d=d):
-                pltpu.make_async_remote_copy(
-                    src_ref=own,
-                    dst_ref=fb.at[pl.ds(place + row, 2)],
-                    send_sem=sendh.at[d],
-                    recv_sem=recvh.at[d],
-                    device_id=to,
-                    device_id_type=MESH,
-                ).start()
-
-            if inner and cross:
-                go()
-            elif inner:
-                pl.when(zc != edge)(go)
-            else:
-                pl.when(zc == edge)(go)
+    def send_near(m):
+        row = 2 * turned(m, 15, core)
+        pltpu.make_async_remote_copy(
+            src_ref=fb.at[pl.ds(BINS + row, 2)],
+            dst_ref=fb.at[pl.ds(2 * BINS * core + row, 2)],
+            send_sem=sendn,
+            recv_sem=recvn,
+            device_id=near,
+            device_id_type=MESH,
+        ).start()
+
+    def send_far(m):
+        row = 2 * turned(m, 15, core)
+        pltpu.make_async_remote_copy(
+            src_ref=fb.at[pl.ds(BINS + row, 2)],
+            dst_ref=lb.at[pl.ds(2 * m, 2)],
+            send_sem=sendf,
+            recv_sem=recvf.at[lax.div(m, 4)],
+            device_id=far,
+            device_id_type=MESH,
+        ).start()
 
     flat = db.reshape(HALVES * HALVES * QROWS, 128)
     for part in range(HALVES):
         for half in range(HALVES):
             landed = db.at[pl.ds((2 * half + part) * 128, 128)]
             pltpu.make_async_copy(landed, landed, recvy.at[2 * half + part]).wait()
+
         if part == 1:
-            for z in range(8):
-                send_halo(2 * z, False, True)
-
-        def azimuth(n, part=part):
+            @pl.when(leaves)
+            def _():
+                def late(m, _):
+                    send_far(m)
+                    return 0
+
+                lax.fori_loop(0, 8, late, 0)
+
+        def azimuth(m, part=part):
+            s = turned(m - 8 * part, 7, core)
             cols = []
             for half in range(HALVES):
-                base = (2 * half + part) * QROWS + n
+                base = (2 * half + part) * QROWS + s
                 re = flat[pl.ds(base, 128, stride=16), :]
                 im = flat[pl.ds(base + 8, 128, stride=16), :]
                 cols.append(jnp.concatenate([re, im], axis=0))
             out_pair = dft_pair(wq, wf, jnp.concatenate(cols, axis=1), tw_az, False, mixed=True)
-            row = BINS + part * HB + n
+            row = BINS + 2 * turned(m, 15, core)
             fb[row] = out_pair[:, :128]
-            fb[row + 8] = out_pair[:, 128:]
+            fb[row + 1] = out_pair[:, 128:]
 
         def azimuth_two(n, _, part=part, azimuth=azimuth):
-            azimuth(2 * n)
-            azimuth(2 * n + 1)
-            send_halo(part * HB + 2 * n, True, part == 1)
-            send_halo(part * HB + 2 * n + 8, True, part == 1)
-            return 0
-
-        lax.fori_loop(0, HB // 4, azimuth_two, 0)
-
-    for d, place in ((0, 0), (1, 2 * BINS)):
-        landed = fb.at[pl.ds(place, BINS)]
-        pltpu.make_async_copy(landed, landed, recvh.at[d]).wait()
-
-    @pl.when(r == 0)
-    def _():
-        def clear(n, _):
-            fb[n] = jnp.zeros((256, 128), F32)
-            return 0
-
-        lax.fori_loop(0, BINS, clear, 0)
-
-    @pl.when(r == NDEV - 1)
-    def _():
-        def clear(n, _):
-            fb[2 * BINS + n] = jnp.zeros((256, 128), F32)
-            return 0
-
-        lax.fori_loop(0, BINS, clear, 0)
+            m = 8 * part + 2 * n
+            azimuth(m)
+            azimuth(m + 1)
+            for k in range(2):
+                send_near(m + k)
+                if part == 1:
+                    send_far(m + k)
+                else:
+                    pl.when(jnp.logical_not(leaves))(functools.partial(send_far, m + k))
+            return 0
+
+        lax.fori_loop(0, 4, azimuth_two, 0)
+
+    others = fb.at[pl.ds(0, BINS)]
+    pltpu.make_async_copy(others, others, recvn).wait()
+    outside = jnp.logical_or(r + core == 0, r + core == NDEV)
 
     def focus(n, mb):
         for m in range(2):
@@ -520,19 +535,29 @@
                 base = (c * 4 + lax.div(b, 8)) * 1024 + lax.rem(b, 8)
                 ub[pl.ds(base, 128, stride=8), :] = y[128 * c : 128 * c + 128, 128 * m : 128 * m + 128]
 
-    def focus_two(n, _):
-        focus(2 * n, mb.at[0])
-        focus(2 * n + 1, mb.at[1])
-        return 0
-
-    outs = []
-    for t in range(4):
-        lax.fori_loop(2 * t, 2 * t + 2, focus_two, 0)
+    for group in range(4):
+        rows = lb.at[pl.ds(8 * group, 8)]
+        pltpu.make_async_copy(rows, rows, recvf.at[group]).wait()
+
+        def move(n, _, group=group):
+            m = 4 * group + n
+            row = 2 * turned(m, 15, 1 - core) + 2 * BINS * core
+            for k in range(2):
+                fb[row + k] = jnp.where(outside, 0.0, lb[2 * m + k])
+            return 0
+
+        lax.fori_loop(0, 4, move, 0)
+
+        def focus_two(n, _, group=group):
+            for k in range(2):
+                focus(turned(4 * group + 2 * n + k, 15, 1 - core), mb.at[k])
+            return 0
+
+        lax.fori_loop(0, 2, focus_two, 0)
+        eight = turned(group, 3, 1 - core)
         for c in range(2):
-            rows = pl.ds((c * 4 + t) * 1024, 1024)
-            copy = pltpu.make_async_copy(ub.at[rows, :], out.at[rows, :], sem_out.at[2 * t + c])
-            copy.start()
-            outs.append(copy)
+            rows = pl.ds(pl.multiple_of((c * 4 + eight) * 1024, 1024), 1024)
+            pltpu.make_async_copy(ub.at[rows, :], out.at[rows, :], sem_out.at[2 * group + c]).start()
 
     for ch in range(CHUNKS):
         gone = xb.at[pl.ds(0, NR - 1), :, pl.ds(ch * CL, CL), :]
@@ -542,16 +567,16 @@
         pltpu.make_async_copy(gone, gone, sendz.at[quarter]).wait()
         gone = eb.at[pl.ds(0, COL), pl.ds(0, (PLANE - 1) * 16), :]
         pltpu.make_async_copy(gone, gone, sendy.at[quarter]).wait()
-    for d in range(2):
-        gone = fb.at[pl.ds(0, BINS)]
-        pltpu.make_async_copy(gone, gone, sendh.at[d]).wait()
-    for copy in outs:
-        copy.wait()
+    gone = fb.at[pl.ds(BINS, BINS)]
+    pltpu.make_async_copy(gone, gone, sendn).wait()
+    pltpu.make_async_copy(gone, gone, sendf).wait()
+    for n in range(8):
+        rows = pl.ds(1024 * n, 1024)
+        pltpu.make_async_copy(ub.at[rows, :], out.at[rows, :], sem_out.at[n]).wait()
 
 
 def local(raw_echo, chirp_spectrum, azimuth_rate, shift_table, filter_index, tap_table):
-    wf, wi, wft, wq, tw_in, tw_out, tw_az = tables()
-    chirp = chirp_spectrum.reshape(2, 128, 32).transpose(0, 2, 1) * (1.0 / NRG)
+    wf, wi, wft, wr, wq, tw_in, tw_out, tw_az = tables()
     vmem = pl.BlockSpec(memory_space=pltpu.VMEM)
     smem = pl.BlockSpec(memory_space=pltpu.SMEM)
     hbm = pl.BlockSpec(memory_space=pl.ANY)
@@ -559,7 +584,7 @@
     image = pl.pallas_call(
         kernel,
         out_shape=jax.ShapeDtypeStruct((8192, 128), F32),
-        in_specs=[hbm, vmem, hbm, vmem, vmem, vmem, vmem, vmem, vmem, smem, smem, smem, smem],
+        in_specs=[hbm, vmem, hbm, vmem, vmem, vmem, vmem, vmem, vmem, vmem, smem, smem, smem, smem],
         out_specs=hbm,
         scratch_shapes=[
             pltpu.VMEM((NR, 2, LINES, 512), F32),
@@ -568,10 +593,12 @@
             pltpu.VMEM((4 * COL, 256, 128), F32),
             pltpu.VMEM((512, 16, 128), F32),
             pltpu.VMEM((3 * BINS, 256, 128), F32),
+            pltpu.VMEM((BINS, 256, 128), F32),
             pltpu.VMEM((BINS, 2, 128, 128), F32),
             pltpu.VMEM((32, 2, 64, 128), F32),
             pltpu.VMEM((2, 256, 256), F32),
             pltpu.VMEM((128, 128), F32),
+            pltpu.VMEM((2, 32, 128), F32),
             dma,
             dma((CHUNKS,)),
             dma((CHUNKS,)),
@@ -579,8 +606,10 @@
             dma((4,)),
             dma((4,)),
             dma((4,)),
-            dma((2,)),
-            dma((2,)),
+            dma,
+            dma,
+            dma,
+            dma((4,)),
             dma((8,)),
         ],
         compiler_params=pltpu.CompilerParams(
@@ -591,7 +620,7 @@
         ),
         name="focus_slab",
     )(
-        raw_echo, chirp, tw_out, wf, wi, wft, wq, tw_in, tw_az,
+        raw_echo, chirp_spectrum, tw_out, wf, wi, wft, wr, wq, tw_in, tw_az,
         azimuth_rate, shift_table, filter_index, tap_table.T,
     )
     image = image.reshape(2, 4, 128, 8, 128).transpose(0, 1, 3, 2, 4)

time: 176 us -> 166 us (0.943)
  Pallas kernels: 169 us -> 160 us
    pallas_call x1, Pallas kernels: 169 us -> 160 us  [local(): pl.pallas_call(kernel, out_shape=jax.ShapeDtypeStruct((8192, 128), F32),...]
where the time goes in v3:
time: 166 us; the launch traced here: 165 us
  Pallas kernels  160 us (96%)
  local copies, waits for them, and re-layouts  4.5 us (3%)
    pallas_call x1, Pallas kernels, local(): pl.pallas_call(kernel, out_shape=jax.ShapeDtypeStruct((8192, 128), F32),...  160 us
    unnamed x1, local copies, waits for them, and re-layouts  4.5 us

profile of v3, /device:TPU:16, one launch (start us, length us, event | category | flops | bytes accessed | tf_op | source)
XLA Modules:
  0.0 164.7 jit_solution(11435990677162948710)
XLA Ops:
  0.0 160.1 %focus_slab.1 = f32[8192,128]{1,0:T(8,128)} custom-call(f32[2,1024,512]{2,1,0:T(8,128)} %raw.1, f32[2,4096]{1,0:T(2,128)} %spectrum.1, f32[32,2,64,128]{3,2,1,0:T(8,128)} %constant.16.clone.tw_out_hbm, bf16[256,768]{1,0:T(8,128)(2,1)} %constant.17.clone.wf, bf16[256,768]{1,0:T(8,128)(2,1)} %constant.18.clone.wi, bf16[768,256]{1,0:T(8,128)(2,1)} %constant.19.clone.wft, ...), custom_call_target="tpu_custom_call" | custom-call | flops 10000000000 | bytes 16777216 | tf_op jit(solution)/shard_map/focus_slab/pallas_call | solution.py:584
  160.2 4.5 %copy.16 = f32[2,32,16384]{2,1,0:T(8,128)} copy(f32[2,32,16384]{2,1,0:T(8,128)} %bitcast.6) | data formatting | bytes 8388608

commit v4 on v3

--- a/solution.py
+++ b/solution.py
@@ -187,9 +187,10 @@
 
 
 def kernel(
-    raw, spectrum, tw_out_hbm, wf, wi, wft, wr, wq, tw_in, tw_az, rate, shift, filt, taps,
+    raw, spectrum_hbm, tw_out_hbm, wf_hbm, wi_hbm, wft_hbm, wr_hbm, wq_hbm, tw_in_hbm, tw_az_hbm, rate, shift, filt, taps,
     out,
     xb, ub, cb, eb, db, fb, lb, pb, twb, mb, c2b, chirp,
+    spectrum, wf, wi, wft, wr, wq, tw_in, tw_az, sem_in,
     sem_tw, send1, recv1, sendz, recvz, sendy, recvy, sendn, recvn, sendf, recvf, sem_out,
 ):
     i = lax.axis_index("rng")
@@ -266,6 +267,18 @@
 
     tw_copy = pltpu.make_async_copy(tw_out_hbm, twb, sem_tw)
     tw_copy.start()
+    loads = [
+        pltpu.make_async_copy(source, place, sem_in.at[n])
+        for n, (source, place) in enumerate(
+            (
+                (spectrum_hbm, spectrum), (wft_hbm, wft), (tw_in_hbm, tw_in), (wr_hbm, wr),
+                (wq_hbm, wq), (wf_hbm, wf), (tw_az_hbm, tw_az), (wi_hbm, wi),
+            )
+        )
+    ]
+    for load in loads:
+        load.start()
+    loads[0].wait()
 
     for part in range(2):
         rows = [spectrum[part : part + 1, 128 * n : 128 * n + 128] for n in range(32)]
@@ -426,6 +439,8 @@
             landed.at[:, pl.ds(pl.multiple_of(yx * 16, 16), 16), :], place, recvy.at[quarter]
         ).start()
 
+    for load in loads[1:]:
+        load.wait()
     first_two(0)
     first_two(1)
     tw_copy.wait()
@@ -459,7 +474,7 @@
             src_ref=fb.at[pl.ds(BINS + row, 2)],
             dst_ref=lb.at[pl.ds(2 * m, 2)],
             send_sem=sendf,
-            recv_sem=recvf.at[lax.div(m, 4)],
+            recv_sem=recvf.at[lax.div(m, 2)],
             device_id=far,
             device_id_type=MESH,
         ).start()
@@ -535,29 +550,22 @@
                 base = (c * 4 + lax.div(b, 8)) * 1024 + lax.rem(b, 8)
                 ub[pl.ds(base, 128, stride=8), :] = y[128 * c : 128 * c + 128, 128 * m : 128 * m + 128]
 
-    for group in range(4):
-        rows = lb.at[pl.ds(8 * group, 8)]
+    for group in range(8):
+        rows = lb.at[pl.ds(4 * group, 4)]
         pltpu.make_async_copy(rows, rows, recvf.at[group]).wait()
-
-        def move(n, _, group=group):
-            m = 4 * group + n
+        for k in range(2):
+            m = 2 * group + k
             row = 2 * turned(m, 15, 1 - core) + 2 * BINS * core
-            for k in range(2):
-                fb[row + k] = jnp.where(outside, 0.0, lb[2 * m + k])
-            return 0
-
-        lax.fori_loop(0, 4, move, 0)
-
-        def focus_two(n, _, group=group):
-            for k in range(2):
-                focus(turned(4 * group + 2 * n + k, 15, 1 - core), mb.at[k])
-            return 0
-
-        lax.fori_loop(0, 2, focus_two, 0)
-        eight = turned(group, 3, 1 - core)
-        for c in range(2):
-            rows = pl.ds(pl.multiple_of((c * 4 + eight) * 1024, 1024), 1024)
-            pltpu.make_async_copy(ub.at[rows, :], out.at[rows, :], sem_out.at[2 * group + c]).start()
+            for h in range(2):
+                fb[row + h] = jnp.where(outside, 0.0, lb[2 * m + h])
+        for k in range(2):
+            focus(turned(2 * group + k, 15, 1 - core), mb.at[k])
+        if group % 2 == 1:
+            eight = turned(group // 2, 3, 1 - core)
+            for c in range(2):
+                rows = pl.ds(pl.multiple_of((c * 4 + eight) * 1024, 1024), 1024)
+                sem = sem_out.at[group - 1 + c]
+                pltpu.make_async_copy(ub.at[rows, :], out.at[rows, :], sem).start()
 
     for ch in range(CHUNKS):
         gone = xb.at[pl.ds(0, NR - 1), :, pl.ds(ch * CL, CL), :]
@@ -577,14 +585,13 @@
 
 def local(raw_echo, chirp_spectrum, azimuth_rate, shift_table, filter_index, tap_table):
     wf, wi, wft, wr, wq, tw_in, tw_out, tw_az = tables()
-    vmem = pl.BlockSpec(memory_space=pltpu.VMEM)
     smem = pl.BlockSpec(memory_space=pltpu.SMEM)
     hbm = pl.BlockSpec(memory_space=pl.ANY)
     dma = pltpu.SemaphoreType.DMA
     image = pl.pallas_call(
         kernel,
         out_shape=jax.ShapeDtypeStruct((8192, 128), F32),
-        in_specs=[hbm, vmem, hbm, vmem, vmem, vmem, vmem, vmem, vmem, vmem, smem, smem, smem, smem],
+        in_specs=[hbm] * 10 + [smem] * 4,
         out_specs=hbm,
         scratch_shapes=[
             pltpu.VMEM((NR, 2, LINES, 512), F32),
@@ -599,6 +606,15 @@
             pltpu.VMEM((2, 256, 256), F32),
             pltpu.VMEM((128, 128), F32),
             pltpu.VMEM((2, 32, 128), F32),
+            pltpu.VMEM((2, NRG), F32),
+            pltpu.VMEM((256, 768), BF16),
+            pltpu.VMEM((256, 768), BF16),
+            pltpu.VMEM((768, 256), BF16),
+            pltpu.VMEM((256, 768), BF16),
+            pltpu.VMEM((256, 768), BF16),
+            pltpu.VMEM((2, 32, 8, 128), F32),
+            pltpu.VMEM((2, 128, 128), F32),
+            dma((8,)),
             dma,
             dma((CHUNKS,)),
             dma((CHUNKS,)),
@@ -609,7 +625,7 @@
             dma,
             dma,
             dma,
-            dma((4,)),
+            dma((8,)),
             dma((8,)),
         ],
         compiler_params=pltpu.CompilerParams(

time: 166 us -> 164 us (0.988)
  Pallas kernels: 160 us -> 158 us
    pallas_call x1, Pallas kernels: 160 us -> 158 us  [local(): pl.pallas_call(kernel, out_shape=jax.ShapeDtypeStruct((8192, 128), F32),...]
where the time goes in v4:
time: 164 us; the launch traced here: 163 us
  Pallas kernels  158 us (96%)
  local copies, waits for them, and re-layouts  4.5 us (3%)
    pallas_call x1, Pallas kernels, local(): pl.pallas_call(kernel, out_shape=jax.ShapeDtypeStruct((8192, 128), F32),...  158 us
    unnamed x1, local copies, waits for them, and re-layouts  4.5 us

profile of v4, /device:TPU:16, one launch (start us, length us, event | category | flops | bytes accessed | tf_op | source)
XLA Modules:
  0.0 162.6 jit_solution(2757472459017164270)
XLA Ops:
  0.0 158.1 %focus_slab.1 = f32[8192,128]{1,0:T(8,128)} custom-call(f32[2,1024,512]{2,1,0:T(8,128)} %raw.1, f32[2,4096]{1,0:T(2,128)} %spectrum_hbm.1, f32[32,2,64,128]{3,2,1,0:T(8,128)} %constant.16.clone.tw_out_hbm, bf16[256,768]{1,0:T(8,128)(2,1)} %constant.17.clone.wf_hbm, bf16[256,768]{1,0:T(8,128)(2,1)} %constant.18.clone.wi_hbm, ...), custom_call_target="tpu_custom_call" | custom-call | flops 10000000000 | bytes 16777216 | tf_op jit(solution)/shard_map/focus_slab/pallas_call | solution.py:591
  158.1 4.5 %copy.16 = f32[2,32,16384]{2,1,0:T(8,128)} copy(f32[2,32,16384]{2,1,0:T(8,128)} %bitcast.6) | data formatting | bytes 8388608

commit v5 on v4

--- a/solution.py
+++ b/solution.py
@@ -450,9 +450,9 @@
     first_two(2)
     forward(0, 0)
     first_two(3)
-    forward(0, 1)
     third(1)
     fourth(1, 0)
+    forward(0, 1)
     fourth(1, 1)
     forward(1, 0)
     forward(1, 1)

time: 164 us -> 162 us (0.988)
  the two profiles are of different devices: /device:TPU:16 before, /device:TPU:6 now
where the time goes in v5:
time: 162 us
  Pallas kernels  158 us (98%)
  local copies, waits for them, and re-layouts  4.5 us (3%)
    pallas_call x1, Pallas kernels, local(): pl.pallas_call(kernel, out_shape=jax.ShapeDtypeStruct((8192, 128), F32),...  158 us
    unnamed x1, local copies, waits for them, and re-layouts  4.5 us

profile of v5, /device:TPU:6, one launch (start us, length us, event | category | flops | bytes accessed | tf_op | source)
XLA Modules:
  0.0 162.0 jit_solution(17982570526145853429)
XLA Ops:
  0.0 157.5 %focus_slab.1 = f32[8192,128]{1,0:T(8,128)} custom-call(f32[2,1024,512]{2,1,0:T(8,128)} %raw.1, f32[2,4096]{1,0:T(2,128)} %spectrum_hbm.1, f32[32,2,64,128]{3,2,1,0:T(8,128)} %constant.16.clone.tw_out_hbm, bf16[256,768]{1,0:T(8,128)(2,1)} %constant.17.clone.wf_hbm, bf16[256,768]{1,0:T(8,128)(2,1)} %constant.18.clone.wi_hbm, ...), custom_call_target="tpu_custom_call" | custom-call | flops 10000000000 | bytes 16777216 | tf_op jit(solution)/shard_map/focus_slab/pallas_call | solution.py:591
  157.5 4.5 %copy.16 = f32[2,32,16384]{2,1,0:T(8,128)} copy(f32[2,32,16384]{2,1,0:T(8,128)} %bitcast.6) | data formatting | bytes 8388608
